TPU v7x, 32 devices: a whole 2x2x4 slice. The times are simulated.
32 devices in a mesh: grp: 2 (over y), tm: 16 (over z, x, core).
Axes of the slice: x: 2, y: 2, z: 4, core: 2. Of those that a mesh axis runs over, the one named last changes fastest.
Arguments:
- initial_weights: float32 [512], replicated, may hold values from 0.1 to 1
- leave_rate: float32 [512], replicated, may hold values from 0.001 to 0.5
- block_weights: float32 [4, 2, 128, 128], replicated, may hold values from 0.1 to 1
- block_cols: int32 [4, 2], replicated, may hold values from 0 to 3, as said below
- emission_weights: float32 [4, 512], replicated, may hold values from 0.02 to 1
- symbols: int32 [768], P(('grp', 'tm')), parts along dimension 0, may hold values from 0 to 3
Outputs:
- occupancy: float32 [768, 512], P(('grp', 'tm')), parts along dimension 0
- log_norm: float32 [768], P(('grp', 'tm')), parts along dimension 0
There are 2 independent parts, one for each index of `grp`. A program takes and returns all parts, laid end to end along the dimension named above; an argument that names none is the same for every part. Nothing has to cross between parts.
Inputs may be any that keep to these rules, and one draw needn't show every extreme that they name: Row r of block_cols holds 2 different block columns, the first of them r.
All inputs are finite; a program needn't handle non-finite values.
Results may differ from a plain program's by a relative error of at most 0.0003.
Values sent between devices are 32-bit elements; how exact they have to be, the bound alone decides.
A program may use at most 64 MiB of HBM per device.

v0:
```python
import jax
import jax.numpy as jnp
from jax import lax
from jax.sharding import PartitionSpec as P

exact_mode = lax.Precision.HIGHEST


def passed_along(value, axis, by):
    devices = lax.axis_size(axis)
    pairs = [(i, i + by) for i in range(devices) if 0 <= i + by < devices]
    return lax.ppermute(value, axis, pairs)


def normalized(matrix):
    return matrix / jnp.sum(matrix)


def joined_product(first_factor, second_factor):
    return normalized(jnp.dot(first_factor, second_factor, precision=exact_mode))


def apply_right(matrix, leave_rate, normed, placement):
    block_rows, block_size = (normed.shape[0], normed.shape[2])
    scaled = (matrix * leave_rate[None, :]).reshape(matrix.shape[0], block_rows, block_size)
    partial_terms = jnp.einsum("xrb,rkbj->xrkj", scaled, normed, precision=exact_mode)
    carried = jnp.einsum("xrkj,rkc->xcj", partial_terms, placement, precision=exact_mode)
    return matrix * (1.0 - leave_rate)[None, :] + carried.reshape(matrix.shape)


def apply_left(vectors, leave_rate, normed, placement):
    block_rows, block_size = (normed.shape[0], normed.shape[2])
    pieces = vectors.reshape(vectors.shape[0], block_rows, block_size)
    gathered = jnp.einsum("rkc,xcj->xrkj", placement, pieces, precision=exact_mode)
    carried = jnp.einsum("rkbj,xrkj->xrb", normed, gathered, precision=exact_mode)
    return vectors * (1.0 - leave_rate)[None, :] + leave_rate[None, :] * carried.reshape(
        vectors.shape
    )


def body(initial_weights, leave_rate, block_weights, block_cols, emission_weights, symbols):
    block_rows = block_weights.shape[0]
    states = leave_rate.shape[0]
    placement = (
        block_cols[:, :, None] == jnp.arange(block_rows, dtype=jnp.int32)[None, None, :]
    ).astype(jnp.float32)
    row_totals = jnp.sum(block_weights, axis=(1, 3))
    normed = block_weights / row_totals[:, None, :, None]
    symbol_count = emission_weights.shape[0]
    emission = emission_weights / jnp.sum(emission_weights, axis=0, keepdims=True)
    indicator = (symbols[:, None] == jnp.arange(symbol_count, dtype=jnp.int32)[None, :]).astype(
        jnp.float32
    )
    emission_rows = jnp.dot(indicator, emission, precision=exact_mode)
    steps_here = symbols.shape[0]

    def build_step(step_index, matrix):
        row_probs = lax.dynamic_slice_in_dim(emission_rows, step_index, 1, 0)
        return normalized(apply_right(matrix, leave_rate, normed, placement) * row_probs)

    local_product = lax.fori_loop(0, steps_here, build_step, jnp.eye(states, dtype=jnp.float32))
    start_vector = (initial_weights / jnp.sum(initial_weights))[None, :]
    final_vector = jnp.full((states, 1), 1.0 / states, jnp.float32)
    position = lax.axis_index("tm")
    device_count = lax.axis_size("tm")
    levels = device_count.bit_length() - 1
    identity = jnp.eye(states, dtype=jnp.float32)
    earlier_total = passed_along(local_product, "tm", 1)
    earlier_total = jnp.where(position >= 1, earlier_total, identity)
    later_total = passed_along(local_product, "tm", -1)
    later_total = jnp.where(position + 1 < device_count, later_total, identity)
    for bit_number in range(levels):
        distance = 2**bit_number
        received = passed_along(earlier_total, "tm", distance)
        received = jnp.where(position >= distance, received, identity)
        earlier_total = joined_product(received, earlier_total)
        arriving = passed_along(later_total, "tm", -distance)
        arriving = jnp.where(position + distance < device_count, arriving, identity)
        later_total = joined_product(later_total, arriving)
    entry_vector = normalized(jnp.dot(start_vector, earlier_total, precision=exact_mode))
    exit_vector = normalized(jnp.dot(later_total, final_vector, precision=exact_mode))

    def forward_step(previous, row_probs):
        unscaled = apply_right(previous[None, :], leave_rate, normed, placement)[0] * row_probs
        normalizer = jnp.sum(unscaled)
        scaled = unscaled / normalizer
        return (scaled, (scaled, jnp.log(normalizer)))

    final_forward, (forward_vectors, log_norm) = lax.scan(
        forward_step, entry_vector[0], emission_rows
    )

    def backward_step(following, row_probs):
        unscaled = apply_left((row_probs * following)[None, :], leave_rate, normed, placement)[0]
        scaled = unscaled / jnp.sum(unscaled)
        return (scaled, scaled)

    last_vector = exit_vector[:, 0]
    final_backward, earlier_vectors = lax.scan(
        backward_step, last_vector, emission_rows[1:], reverse=True
    )
    backward_vectors = jnp.concatenate([earlier_vectors, last_vector[None, :]], axis=0)
    joint_terms = forward_vectors * backward_vectors
    occupancy = states * joint_terms / jnp.sum(joint_terms, axis=1, keepdims=True)
    return (occupancy, log_norm)


def solution(mesh):
    placed = (P(), P(), P(), P(), P(), P(("grp", "tm")))
    return jax.shard_map(
        body,
        mesh=mesh,
        in_specs=placed,
        out_specs=(P(("grp", "tm"), None), P(("grp", "tm"))),
        check_vma=False,
    )
```

profile of v0, /device:TPU:0, one launch (start us, length us, event | category | flops | bytes accessed | tf_op | source)
XLA Modules:
  0.0 592.3 jit_solution(6106600097537884815)
XLA Ops:
  3.4 247.4 %while.46 = (s32[]{:T(128)}, f32[512,512]{1,0:T(8,128)S(1)}, f32[512]{0:T(512)S(1)}, f32[4,2,128,128]{3,2,1,0:T(8,128)S(1)}, f32[24,512]{1,0:T(8,128)S(1)}, /*index=5*/s32[4,2]{0,1:T(2,128)S(1)}, s32[]{:T(128)}) while((s32[]{:T(128)}, f32[512,512]{1,0:T(8,128)S(1)}, f32[512]{0:T(512)S(1)}, f32[4,2,128,128]{3,2,1,0:T(8,128)S(1)}, ...), condition=%wide.region_5.0_spmd.clone, body=%wide.region_3.5_spmd.clone.sunk | while | flops 832832064 | bytes 16271481 | solution.py:61
  8.0 3.7 fusion.101
  28.6 3.7 fusion.101
  49.2 3.7 fusion.101
  69.8 3.7 fusion.101
  80.1 3.7 fusion.101
  90.4 3.7 fusion.101
  100.7 3.7 fusion.101
  111.0 3.7 fusion.101
  121.3 3.7 fusion.101
  131.6 3.7 fusion.101
  142.0 3.7 fusion.101
  152.3 3.7 fusion.101
  172.9 3.7 fusion.101
  193.5 3.7 fusion.101
  214.1 3.7 fusion.101
  224.4 3.7 fusion.101
  234.7 3.7 fusion.101
  245.0 3.7 fusion.101
  259.3 34.7 %collective-permute-start.1 = (f32[512,512]{1,0:T(8,128)S(1)}, f32[512,512]{1,0:T(8,128)}, u32[]{:S(2)}, u32[]{:S(2)}) collective-permute-start(f32[512,512]{1,0:T(8,128)S(1)} %convert_select_fusion.9), channel_id=1, source_target_pairs={{0,1},{1,2},{2,3},{3,4},{4,5},{5,6},{6,7},{7,8},{8,9},{9,10},{10,1... | collective-permute-start | bytes 3145736 | tf_op jit(solution)/shard_map/ppermute | solution.py:12
  294.0 4.2 fusion.63
  304.7 35.0 %collective-permute-start.2 = (f32[512,512]{1,0:T(8,128)S(1)}, f32[512,512]{1,0:T(8,128)}, u32[]{:S(2)}, u32[]{:S(2)}) collective-permute-start(f32[512,512]{1,0:T(8,128)S(1)} %broadcast_divide_fusion.8), channel_id=1, source_target_pairs={{0,2},{1,3},{2,4},{3,5},{4,6},{5,7},{6,8},{7,9},{8,10},{9,11},{10,... | collective-permute-start | bytes 3145736 | tf_op jit(solution)/shard_map/ppermute | solution.py:12
  339.7 4.2 fusion.64
  345.9 12.5 %collective-permute-done.2 = f32[512,512]{1,0:T(8,128)} collective-permute-done((f32[512,512]{1,0:T(8,128)S(1)}, f32[512,512]{1,0:T(8,128)}, u32[]{:S(2)}, u32[]{:S(2)}) %collective-permute-start.2) | collective-permute-done | bytes 1048608 | tf_op jit(solution)/shard_map/ppermute | solution.py:12
  361.9 10.1 %collective-permute-start.3 = (f32[512,512]{1,0:T(8,128)S(1)}, f32[512,512]{1,0:T(8,128)}, u32[]{:S(2)}, u32[]{:S(2)}) collective-permute-start(f32[512,512]{1,0:T(8,128)S(1)} %broadcast_divide_fusion.7), channel_id=1, source_target_pairs={{0,4},{1,5},{2,6},{3,7},{4,8},{5,9},{6,10},{7,11},{8,12},{9,13},{1... | collective-permute-start | bytes 3145736 | tf_op jit(solution)/shard_map/ppermute | solution.py:12
  372.0 16.1 %collective-permute-done.8 = f32[512,512]{1,0:T(8,128)} collective-permute-done((f32[512,512]{1,0:T(8,128)S(1)}, f32[512,512]{1,0:T(8,128)}, u32[]{:S(2)}, u32[]{:S(2)}) %collective-permute-start.8) | collective-permute-done | bytes 1048608 | tf_op jit(solution)/shard_map/ppermute | solution.py:12
  388.1 3.9 fusion.65
  398.7 14.7 %collective-permute-start.4 = (f32[512,512]{1,0:T(8,128)S(1)}, f32[512,512]{1,0:T(8,128)}, u32[]{:S(2)}, u32[]{:S(2)}) collective-permute-start(f32[512,512]{1,0:T(8,128)S(1)} %broadcast_divide_fusion.6), channel_id=1, source_target_pairs={{0,8},{1,9},{2,10},{3,11},{4,12},{5,13},{6,14},{7,15},{16,24},{17,... | collective-permute-start | bytes 3145736 | tf_op jit(solution)/shard_map/ppermute | solution.py:12
  413.5 36.4 %collective-permute-done.9 = f32[512,512]{1,0:T(8,128)} collective-permute-done((f32[512,512]{1,0:T(8,128)S(1)}, f32[512,512]{1,0:T(8,128)}, u32[]{:S(2)}, u32[]{:S(2)}) %collective-permute-start.9) | collective-permute-done | bytes 1048608 | tf_op jit(solution)/shard_map/ppermute | solution.py:12
  449.8 3.9 fusion.66
  456.6 48.3 %while.48 = (s32[]{:T(128)}, f32[512]{0:T(512)S(1)}, f32[23,512]{1,0:T(8,128)S(1)}, f32[23,512]{1,0:T(8,128)S(1)}, f32[512]{0:T(512)S(1)}, /*index=5*/f32[4,2,12...) while((s32[]{:T(128)}, f32[512]{0:T(512)S(1)}, ...), condition=%wide.region_21.22_spmd.clone, body=%wide.region_19.21_spmd.clone.sunk | while | flops 1626178 | bytes 561313 | solution.py:99
  510.1 81.3 %while.47 = (s32[]{:T(128)}, f32[512]{0:T(512)S(1)}, f32[24,512]{1,0:T(8,128)S(1)}, f32[24]{0:T(128)S(1)}, f32[512]{0:T(512)S(1)}, /*index=5*/f32[4,2,128,128]{3...) while((s32[]{:T(128)}, f32[512]{0:T(512)S(1)}, ...), condition=%wide.region_13.14_spmd.clone, body=%wide.region_11.0_spmd.clone.sunk | while | flops 1626689 | bytes 569521 | solution.py:89
  (561 shorter events, 329.8 us)
Async XLA Ops:
  0.6 2.5 copy-start.2
  0.6 2.6 copy-start.4
  0.7 2.8 copy-start
  0.7 2.8 copy-start.1
  250.8 4.7 collective-permute-start.5
  252.1 7.0 %collective-permute-start = (f32[512,512]{1,0:T(8,128)S(1)}, f32[512,512]{1,0:T(8,128)S(1)}, u32[]{:S(2)}, u32[]{:S(2)}) collective-permute-start(f32[512,512]{1,0:T(8,128)S(1)} %get-tuple-element.295), channel_id=1, source_target_pairs={{0,1},{1,2},{2,3},{3,4},{4,5},{5,6},{6,7},{7,8},{8,9},{9,10},{10,1... | collective-permute-start | bytes 3145736 | tf_op jit(solution)/shard_map/ppermute | solution.py:12
  257.8 36.2 %collective-permute-start.6 = (f32[512,512]{1,0:T(8,128)}, f32[512,512]{1,0:T(8,128)}, u32[]{:S(2)}, u32[]{:S(2)}) collective-permute-start(f32[512,512]{1,0:T(8,128)} %convert_select_fusion.4), channel_id=1, source_target_pairs={{1,0},{2,1},{3,2},{4,3},{5,4},{6,5},{7,6},{8,7},{9,8},{10,9},{11,1... | collective-permute-start | bytes 3145736 | tf_op jit(solution)/shard_map/ppermute | solution.py:12
  259.3 42.0 %collective-permute-start.1 = (f32[512,512]{1,0:T(8,128)S(1)}, f32[512,512]{1,0:T(8,128)}, u32[]{:S(2)}, u32[]{:S(2)}) collective-permute-start(f32[512,512]{1,0:T(8,128)S(1)} %convert_select_fusion.9), channel_id=1, source_target_pairs={{0,1},{1,2},{2,3},{3,4},{4,5},{5,6},{6,7},{7,8},{8,9},{9,10},{10,1... | collective-permute-start | bytes 3145736 | tf_op jit(solution)/shard_map/ppermute | solution.py:12
  300.0 39.7 %collective-permute-start.7 = (f32[512,512]{1,0:T(8,128)}, f32[512,512]{1,0:T(8,128)}, u32[]{:S(2)}, u32[]{:S(2)}) collective-permute-start(f32[512,512]{1,0:T(8,128)} %broadcast_divide_fusion.5), channel_id=1, source_target_pairs={{2,0},{3,1},{4,2},{5,3},{6,4},{7,5},{8,6},{9,7},{10,8},{11,9},{12,... | collective-permute-start | bytes 3145736 | tf_op jit(solution)/shard_map/ppermute | solution.py:12
  304.7 53.7 %collective-permute-start.2 = (f32[512,512]{1,0:T(8,128)S(1)}, f32[512,512]{1,0:T(8,128)}, u32[]{:S(2)}, u32[]{:S(2)}) collective-permute-start(f32[512,512]{1,0:T(8,128)S(1)} %broadcast_divide_fusion.8), channel_id=1, source_target_pairs={{0,2},{1,3},{2,4},{3,5},{4,6},{5,7},{6,8},{7,9},{8,10},{9,11},{10,... | collective-permute-start | bytes 3145736 | tf_op jit(solution)/shard_map/ppermute | solution.py:12
  344.6 43.4 %collective-permute-start.8 = (f32[512,512]{1,0:T(8,128)S(1)}, f32[512,512]{1,0:T(8,128)}, u32[]{:S(2)}, u32[]{:S(2)}) collective-permute-start(f32[512,512]{1,0:T(8,128)S(1)} %broadcast_divide_fusion.4), channel_id=1, source_target_pairs={{4,0},{5,1},{6,2},{7,3},{8,4},{9,5},{10,6},{11,7},{12,8},{13,9},{1... | collective-permute-start | bytes 3145736 | tf_op jit(solution)/shard_map/ppermute | solution.py:12
  361.9 32.2 %copy-start.3 = (f32[512]{0:T(512)S(1)}, f32[512]{0:T(512)}, u32[]{:S(2)}) copy-start(f32[512]{0:T(512)} %param.12) | copy-start | bytes 6148
  361.9 33.4 %collective-permute-start.3 = (f32[512,512]{1,0:T(8,128)S(1)}, f32[512,512]{1,0:T(8,128)}, u32[]{:S(2)}, u32[]{:S(2)}) collective-permute-start(f32[512,512]{1,0:T(8,128)S(1)} %broadcast_divide_fusion.7), channel_id=1, source_target_pairs={{0,4},{1,5},{2,6},{3,7},{4,8},{5,9},{6,10},{7,11},{8,12},{9,13},{1... | collective-permute-start | bytes 3145736 | tf_op jit(solution)/shard_map/ppermute | solution.py:12
  392.7 57.1 %collective-permute-start.9 = (f32[512,512]{1,0:T(8,128)S(1)}, f32[512,512]{1,0:T(8,128)}, u32[]{:S(2)}, u32[]{:S(2)}) collective-permute-start(f32[512,512]{1,0:T(8,128)S(1)} %broadcast_divide_fusion.3), channel_id=1, source_target_pairs={{8,0},{9,1},{10,2},{11,3},{12,4},{13,5},{14,6},{15,7},{24,16},{25,... | collective-permute-start | bytes 3145736 | tf_op jit(solution)/shard_map/ppermute | solution.py:12
  398.7 106.2 %collective-permute-start.4 = (f32[512,512]{1,0:T(8,128)S(1)}, f32[512,512]{1,0:T(8,128)}, u32[]{:S(2)}, u32[]{:S(2)}) collective-permute-start(f32[512,512]{1,0:T(8,128)S(1)} %broadcast_divide_fusion.6), channel_id=1, source_target_pairs={{0,8},{1,9},{2,10},{3,11},{4,12},{5,13},{6,14},{7,15},{16,24},{17,... | collective-permute-start | bytes 3145736 | tf_op jit(solution)/shard_map/ppermute | solution.py:12
  591.4 0.8 copy-start.5
where the time goes:
time: 595 us; the launch traced here: 592 us
  matrix products  206 us (35%)
  other arithmetic  152 us (26%)
  starting transfers between devices  104 us (17%)
  waiting for transfers between devices  65.3 us (11%)
  local copies, waits for them, and re-layouts  44 us (7%)
  loops' own time  19.5 us (3%)
    dot_general x48, matrix products, apply_right(): jnp.einsum('xrkj,rkc->xcj', partial_terms, placement, precision=exact_mode)  108 us
    ppermute x10, starting transfers between devices, passed_along(): return lax.ppermute(value, axis, pairs)  104 us
    ppermute x10, waiting for transfers between devices, passed_along(): return lax.ppermute(value, axis, pairs)  65.3 us
    dot_general x48, matrix products, apply_right(): jnp.einsum('xrb,rkbj->xrkj', scaled, normed, precision=exact_mode)  52.3 us
    reshape x24, local copies, waits for them, and re-layouts, apply_right(): (matrix * leave_rate[None, :]).reshape(matrix.shape[0], block_rows, block...  37.5 us
    div x32, other arithmetic, normalized(): return matrix / jnp.sum(matrix)  33.8 us
    div x48, other arithmetic, forward_step(): scaled = unscaled / normalizer  31.4 us
    mul x48, other arithmetic, apply_right(): matrix * leave_rate[None, :]  27 us
  transfers between devices with their start and end apart: 10, of which 4 were waited for; matrix products, arithmetic and copies ran while one was open for 14% of the time, Pallas kernels for 0%

commit v1 on v0

v1 whole, which is shorter than its diff:
```python
import functools
import jax
import jax.numpy as jnp
from jax import lax
from jax.experimental import pallas as pl
from jax.experimental.pallas import tpu as pltpu
from jax.sharding import PartitionSpec as P

f32 = jnp.float32
bf16 = jnp.bfloat16
SUBS = 4
NN = (((1,), (0,)), ((), ()))
NT = (((1,), (1,)), ((), ()))


def split(x):
    hi = x.astype(bf16)
    return hi, (x - hi.astype(f32)).astype(bf16)


def dot(a, b, dims=NN):
    return lax.dot_general(a, b, dims, preferred_element_type=f32)


def thin(x, hi, lo, dims=NN):
    top = x.astype(bf16).astype(f32)
    both = jnp.concatenate([top, x - top], axis=0).astype(bf16)
    first = dot(both, hi, dims)
    second = dot(both, lo, dims)
    return first[:8] + (first[8:] + second[:8])


def kernel(init_ref, leave_ref, bw_ref, cols_ref, em_ref, sym_ref, occ_ref, ln_ref,
           w_ref, w_hi, w_lo, x_ref, p_hi, p_lo, q_hi, q_lo, e_ref, u_ref, b_ref,
           f_in, f_out, b_in, b_out, f_send, f_recv, b_send, b_recv):
    pos = lax.axis_index("tm")
    count = lax.axis_size("tm")
    nblk, kb, block, _ = bw_ref.shape
    states = nblk * block
    symbols = em_ref.shape[0]
    steps = occ_ref.shape[0]
    per = steps // SUBS

    barrier = pltpu.get_barrier_semaphore()

    @pl.when(pos > 0)
    def _():
        pl.semaphore_signal(barrier, inc=1, device_id={"tm": pos - 1})

    @pl.when(pos < count - 1)
    def _():
        pl.semaphore_signal(barrier, inc=1, device_id={"tm": pos + 1})

    leave = leave_ref[...]
    stay = 1.0 - leave
    leave_col = jnp.transpose(jnp.broadcast_to(leave, (128, states)))
    for r in range(nblk):
        total = jnp.sum(bw_ref[r, 0], axis=1, keepdims=True)
        for k in range(1, kb):
            total = total + jnp.sum(bw_ref[r, k], axis=1, keepdims=True)
        scale = leave_col[r * block:(r + 1) * block, :] / total
        for c in range(nblk):
            acc = bw_ref[r, 0] * jnp.where(cols_ref[r, 0] == c, 1.0, 0.0)
            for k in range(1, kb):
                acc = acc + bw_ref[r, k] * jnp.where(cols_ref[r, k] == c, 1.0, 0.0)
            acc = acc * scale
            hi, lo = split(acc)
            rs = slice(r * block, (r + 1) * block)
            cs = slice(c * block, (c + 1) * block)
            w_ref[rs, cs] = acc
            w_hi[rs, cs] = hi
            w_lo[rs, cs] = lo

    em = em_ref[...]
    em = em / jnp.sum(em, axis=0, keepdims=True)
    e_ref[...] = jnp.zeros_like(e_ref)
    for j in range(per):
        for g in range(SUBS):
            s = sym_ref[g * per + j]
            row = jnp.zeros((1, states), f32)
            for v in range(symbols):
                row = row + em[v:v + 1] * jnp.where(s == v, 1.0, 0.0)
            e_ref[j, g:g + 1, :] = row

    eye = (lax.broadcasted_iota(jnp.int32, (states, states), 0)
           == lax.broadcasted_iota(jnp.int32, (states, states), 1))
    full_step = jnp.where(eye, jnp.broadcast_to(stay, (states, states)), 0.0) + w_ref[...]
    for g in range(SUBS):
        x_ref[g] = full_step * e_ref[0, g:g + 1, :]

    def advance(j, carry):
        for g in range(SUBS):
            x = x_ref[g]
            xb = x.astype(bf16)
            acc = dot(xb, w_hi[...]) + dot(xb, w_lo[...])
            x_ref[g] = (x * stay + acc) * e_ref[j, g:g + 1, :]
        return carry

    lax.fori_loop(1, per, advance, 0)

    for g in range(SUBS):
        x = x_ref[g]
        x = x * (1.0 / jnp.max(x))
        hi, lo = split(x)
        p_hi[g] = hi
        p_lo[g] = lo

    def joined(a, b):
        return dot(a[0], b[0]) + (dot(a[0], b[1]) + dot(a[1], b[0]))

    left = joined((p_hi[0], p_lo[0]), (p_hi[1], p_lo[1]))
    x_ref[0] = left
    right = joined((p_hi[2], p_lo[2]), (p_hi[3], p_lo[3]))
    x_ref[1] = right
    whole = joined(split(x_ref[0]), split(x_ref[1]))
    hi, lo = split(whole * (1.0 / jnp.max(whole)))
    q_hi[...] = hi
    q_lo[...] = lo

    f_copy = pltpu.make_async_remote_copy(
        src_ref=f_out, dst_ref=f_in, send_sem=f_send, recv_sem=f_recv,
        device_id={"tm": lax.rem(pos + 1, count)})
    b_copy = pltpu.make_async_remote_copy(
        src_ref=b_out, dst_ref=b_in, send_sem=b_send, recv_sem=b_recv,
        device_id={"tm": lax.rem(pos + count - 1, count)})

    inner = jnp.logical_and(pos > 0, pos < count - 1)

    @pl.when(inner)
    def _():
        pl.semaphore_wait(barrier, 2)

    @pl.when(jnp.logical_not(inner))
    def _():
        pl.semaphore_wait(barrier, 1)

    def forward_hop():
        @pl.when(pos == 0)
        def _():
            f_in[...] = init_ref[...]

        @pl.when(pos > 0)
        def _():
            f_copy.wait_recv()

        @pl.when(pos < count - 1)
        def _():
            v = f_in[...]
            out = thin(jnp.broadcast_to(v, (8, states)), q_hi[...], q_lo[...])
            f_out[...] = out[0:1] * (1.0 / jnp.sum(v))
            f_copy.start()

    def backward_hop():
        @pl.when(pos == count - 1)
        def _():
            b_in[...] = jnp.full((1, states), 1.0 / states, f32)

        @pl.when(pos < count - 1)
        def _():
            b_copy.wait_recv()

        @pl.when(pos > 0)
        def _():
            w = b_in[...]
            out = thin(jnp.broadcast_to(w, (8, states)), q_hi[...], q_lo[...], NT)
            b_out[...] = out[0:1] * (1.0 / jnp.sum(w))
            b_copy.start()

    @pl.when(2 * pos < count)
    def _():
        forward_hop()
        backward_hop()

    @pl.when(2 * pos >= count)
    def _():
        backward_hop()
        forward_hop()

    def unit(x):
        return x * (1.0 / jnp.sum(x, axis=1, keepdims=True))

    fs = [unit(f_in[...])]
    for g in range(SUBS - 1):
        nxt = thin(jnp.broadcast_to(fs[-1], (8, states)), p_hi[g], p_lo[g])
        fs.append(unit(nxt[0:1]))
    bs = [unit(b_in[...])]
    for g in range(SUBS - 1, 0, -1):
        nxt = thin(jnp.broadcast_to(bs[-1], (8, states)), p_hi[g], p_lo[g], NT)
        bs.append(unit(nxt[0:1]))
    bs = bs[::-1]
    pad = [jnp.zeros((8 - SUBS, states), f32)]
    f = jnp.concatenate(fs + pad, axis=0)
    b = jnp.concatenate(bs + pad, axis=0)
    b_ref[per - 1] = b
    for i in range(per):
        f = (f * stay + thin(f, w_hi[...], w_lo[...])) * e_ref[i]
        u_ref[i] = f
        j = per - 1 - i
        if j > 0:
            m = b * e_ref[j]
            b = m * stay + thin(m, w_hi[...], w_lo[...], NT)
            b_ref[j - 1] = b

    before = jnp.ones((8, 1), f32)
    for i in range(per):
        u = u_ref[i]
        here = jnp.sum(u, axis=1, keepdims=True)
        logs = jnp.log(here / before)
        before = here
        bb = b_ref[i]
        joint = (u / here) * (bb / jnp.sum(bb, axis=1, keepdims=True))
        occ = states * joint / jnp.sum(joint, axis=1, keepdims=True)
        for g in range(SUBS):
            occ_ref[g * per + i:g * per + i + 1, :] = occ[g:g + 1]
            ln_ref[g * per + i:g * per + i + 1, :] = logs[g:g + 1]

    @pl.when(pos < count - 1)
    def _():
        f_copy.wait_send()

    @pl.when(pos > 0)
    def _():
        b_copy.wait_send()


def body(initial_weights, leave_rate, block_weights, block_cols, emission_weights, symbols):
    states = leave_rate.shape[0]
    steps = symbols.shape[0]
    per = steps // SUBS
    vmem = pl.BlockSpec(memory_space=pltpu.VMEM)
    smem = pl.BlockSpec(memory_space=pltpu.SMEM)
    square = (states, states)
    row = pltpu.VMEM((1, states), f32)
    occupancy, log_norm = pl.pallas_call(
        kernel,
        out_shape=(jax.ShapeDtypeStruct((steps, states), f32),
                   jax.ShapeDtypeStruct((steps, 1), f32)),
        in_specs=[vmem, vmem, vmem, smem, vmem, smem],
        out_specs=(vmem, vmem),
        scratch_shapes=[
            pltpu.VMEM(square, f32), pltpu.VMEM(square, bf16), pltpu.VMEM(square, bf16),
            pltpu.VMEM((SUBS,) + square, f32),
            pltpu.VMEM((SUBS,) + square, bf16), pltpu.VMEM((SUBS,) + square, bf16),
            pltpu.VMEM(square, bf16), pltpu.VMEM(square, bf16),
            pltpu.VMEM((per, 8, states), f32), pltpu.VMEM((per, 8, states), f32),
            pltpu.VMEM((per, 8, states), f32),
            row, row, row, row,
            pltpu.SemaphoreType.DMA, pltpu.SemaphoreType.DMA,
            pltpu.SemaphoreType.DMA, pltpu.SemaphoreType.DMA,
        ],
        compiler_params=pltpu.CompilerParams(
            collective_id=0, has_side_effects=True, vmem_limit_bytes=48 * 1024 * 1024),
    )(initial_weights[None, :], leave_rate[None, :], block_weights, block_cols,
      emission_weights, symbols)
    return occupancy, log_norm[:, 0]


def solution(mesh):
    placed = (P(), P(), P(), P(), P(), P(("grp", "tm")))
    return jax.shard_map(
        body,
        mesh=mesh,
        in_specs=placed,
        out_specs=(P(("grp", "tm"), None), P(("grp", "tm"))),
        check_vma=False,
    )
```

time: 595 us -> 59.7 us (0.10)
  matrix products: 206 us -> 0 us
  other arithmetic: 152 us -> 0.63 us
  starting transfers between devices: 104 us -> 0 us
  waiting for transfers between devices: 65.3 us -> 0 us
  Pallas kernels: 0 us -> 54.5 us
  local copies, waits for them, and re-layouts: 44 us -> 3.67 us
  loops' own time: 19.5 us -> 0 us
    dot_general x153 -> x0, matrix products: 206 us -> none  [the longest x48 108 us: apply_right(): jnp.einsum('xrkj,rkc->xcj', partial_terms, placement, precision=exact_mode)]
    ppermute x10 -> x0, starting transfers between devices: 104 us -> none  [passed_along(): return lax.ppermute(value, axis, pairs)]
    div x106 -> x0, other arithmetic: 82.6 us -> none  [the longest x32 33.8 us: normalized(): return matrix / jnp.sum(matrix)]
    ppermute x10 -> x0, waiting for transfers between devices: 65.3 us -> none  [passed_along(): return lax.ppermute(value, axis, pairs)]
    pallas_call x0 -> x1, Pallas kernels: none -> 54.5 us  [body(): pl.pallas_call(kernel, out_shape=(jax.ShapeDtypeStruct((steps, states), f...]
    reduce_sum x53 -> x0, other arithmetic: 39.7 us -> none  [the longest x26 23.5 us: normalized(): return matrix / jnp.sum(matrix)]
    reshape x24 -> x0, local copies, waits for them, and re-layouts: 37.5 us -> none  [apply_right(): (matrix * leave_rate[None, :]).reshape(matrix.shape[0], block_rows, block...]
    mul x48 -> x0, other arithmetic: 27 us -> none  [apply_right(): matrix * leave_rate[None, :]]
  transfers between devices with their start and end apart: 10 -> 0, of which waited for: 4 -> 0; matrix products, arithmetic and copies ran while one was open for 14% -> 0% of each run, Pallas kernels for 0% -> 0%
where the time goes in v1:
time: 59.7 us; the launch traced here: 59.5 us
  Pallas kernels  54.5 us (91%)
  local copies, waits for them, and re-layouts  3.67 us (6%)
  between operations  0.67 us (1%)
  other arithmetic  0.63 us (1%)
    pallas_call x1, Pallas kernels, body(): pl.pallas_call(kernel, out_shape=(jax.ShapeDtypeStruct((steps, states), f...  54.5 us
    unnamed x14, local copies, waits for them, and re-layouts  3.67 us

profile of v1, /device:TPU:0, one launch (start us, length us, event | category | flops | bytes accessed | tf_op | source)
XLA Modules:
  0.0 59.5 jit_solution(9898644529142596484)
XLA Ops:
  0.6 0.0 copy-start.5
  0.6 0.0 copy-start.2
  0.7 0.0 copy-start.3
  0.7 0.7 %copy-done.5 = s32[4,2]{0,1:T(2,128)S(1)} copy-done((s32[4,2]{0,1:T(2,128)S(1)}, s32[4,2]{0,1:T(2,128)}, u32[]{:S(2)}) %copy-start.5) | copy-done | bytes 56
  1.3 0.0 copy-start.4
  1.3 0.1 copy.9.cols_ref
  1.4 0.0 copy-done.2
  1.4 0.0 copy-done.3
  1.4 0.6 copy-done.4
  2.0 0.0 copy-start
  2.0 1.0 %copy-done = f32[4,2,128,128]{3,2,1,0:T(8,128)S(1)} copy-done((f32[4,2,128,128]{3,2,1,0:T(8,128)S(1)}, f32[4,2,128,128]{3,2,1,0:T(8,128)}, u32[]{:S(2)}) %copy-start) | copy-done | bytes 524312
  3.0 0.0 copy-start.1
  3.0 0.7 %copy-done.1 = f32[4,512]{1,0:T(4,128)S(1)} copy-done((f32[4,512]{1,0:T(4,128)S(1)}, f32[4,512]{1,0:T(4,128)}, u32[]{:S(2)}) %copy-start.1) | copy-done | bytes 8216
  3.7 54.5 %shard_map.77 = (f32[24,512]{1,0:T(8,128)S(1)}, f32[24,1]{1,0:T(8,128)S(1)}) custom-call(f32[1,512]{1,0:T(1,128)S(1)} %bitcast.2, f32[1,512]{1,0:T(1,128)S(1)} %bitcast.3, f32[4,2,128,128]{3,2,1,0:T(8,128)S(1)} %copy-done, s32[4,2]{1,0:T(4,128)S(1)} %copy.9.cols_ref, f32[4,512]{1,0:T(4,128)S(1)} %copy-done.1, s32[24]{0:T(128)S(1)} %copy-done.4), custom_call_target="tpu_custom_call" | custom-call | tf_op jit(solution)/shard_map/pallas_call | solution.py:234
  58.3 0.6 %reduce = f32[24]{0:T(128)} reduce(f32[24,1]{1,0:T(8,128)S(1)} %get-tuple-element.5, f32[]{:T(128)} %constant.1), dimensions={1}, to_apply=%get-tuple-element.5.reduce_sub_computation | reduce | bytes 196 | tf_op jit(solution)/shard_map/pallas_call | solution.py:234
  58.9 0.6 %copy.11 = f32[24,512]{1,0:T(8,128)} copy(f32[24,512]{1,0:T(8,128)S(1)} %get-tuple-element.8) | data formatting | bytes 98304
Async XLA Ops:
  0.6 0.7 %copy-start.5 = (s32[4,2]{0,1:T(2,128)S(1)}, s32[4,2]{0,1:T(2,128)}, u32[]{:S(2)}) copy-start(s32[4,2]{0,1:T(2,128)} %param.9) | copy-start | bytes 100
  0.6 0.8 %copy-start.2 = (f32[512]{0:T(512)S(1)}, f32[512]{0:T(512)}, u32[]{:S(2)}) copy-start(f32[512]{0:T(512)} %param.6) | copy-start | bytes 6148
  0.7 0.8 %copy-start.3 = (f32[512]{0:T(512)S(1)}, f32[512]{0:T(512)}, u32[]{:S(2)}) copy-start(f32[512]{0:T(512)} %param.7) | copy-start | bytes 6148
  1.3 0.7 %copy-start.4 = (s32[24]{0:T(128)S(1)}, s32[24]{0:T(128)}, u32[]{:S(2)}) copy-start(s32[24]{0:T(128)} %sym_ref.1) | copy-start | bytes 292
  2.0 1.0 %copy-start = (f32[4,2,128,128]{3,2,1,0:T(8,128)S(1)}, f32[4,2,128,128]{3,2,1,0:T(8,128)}, u32[]{:S(2)}) copy-start(f32[4,2,128,128]{3,2,1,0:T(8,128)} %bw_ref.1) | copy-start | bytes 1572868
  3.0 0.7 %copy-start.1 = (f32[4,512]{1,0:T(4,128)S(1)}, f32[4,512]{1,0:T(4,128)}, u32[]{:S(2)}) copy-start(f32[4,512]{1,0:T(4,128)} %em_ref.1) | copy-start | bytes 24580

commit v2 on v1

v2 whole, which is shorter than its diff:
```python
import functools
import jax
import jax.numpy as jnp
from jax import lax
from jax.experimental import pallas as pl
from jax.experimental.pallas import tpu as pltpu
from jax.sharding import PartitionSpec as P

f32 = jnp.float32
bf16 = jnp.bfloat16
SUBS = 4
NN = (((1,), (0,)), ((), ()))
NT = (((1,), (1,)), ((), ()))


def split(x):
    hi = x.astype(bf16)
    return hi, (x - hi.astype(f32)).astype(bf16)


def dot(a, b, dims=NN):
    return lax.dot_general(a, b, dims, preferred_element_type=f32)


def thin(x, hi, lo, dims=NN):
    top = x.astype(bf16).astype(f32)
    both = jnp.concatenate([top, x - top], axis=0).astype(bf16)
    first = dot(both, hi, dims)
    second = dot(both, lo, dims)
    return first[:8] + (first[8:] + second[:8])


def kernel(init_ref, leave_ref, bw_hbm, cols_hbm, em_hbm, sym_hbm, occ_ref, ln_ref,
           bw_ref, cols_ref, em_ref, sym_ref, in_sems,
           w_ref, w_hi, w_lo, x_ref, p_hi, p_lo, h_hi, h_lo, q_hi, q_lo, e_ref, u_ref, b_ref, l_ref,
           mine, got_cols, got_rows, f_in, f_out, b_in, b_out, f_side, b_side, side_out,
           x_send, x_recv, f_send, f_recv, b_send, b_recv, s_send, s_recv):
    pos = lax.axis_index("tm")
    count = lax.axis_size("tm")
    chips = count // 2
    chip = lax.div(pos, 2)
    core = lax.rem(pos, 2)
    partner = chip * 2 + (1 - core)
    below = lax.rem(chip + chips - 1, chips) * 2
    above = lax.rem(chip + 1, chips) * 2
    nblk, kb, block, _ = bw_ref.shape
    states = nblk * block
    symbols = em_ref.shape[0]
    steps = occ_ref.shape[0]
    per = steps // SUBS
    half = states // 2

    loads = [pltpu.make_async_copy(src, dst, in_sems.at[i]) for i, (src, dst) in enumerate(
        [(bw_hbm, bw_ref), (cols_hbm, cols_ref), (em_hbm, em_ref), (sym_hbm, sym_ref)])]
    for load in loads:
        load.start()

    barrier = pltpu.get_barrier_semaphore()

    pl.semaphore_signal(barrier, inc=1, device_id={"tm": partner})

    @pl.when(chip > 0)
    def _():
        for c in range(2):
            pl.semaphore_signal(barrier, inc=1, device_id={"tm": below + c})

    @pl.when(chip < chips - 1)
    def _():
        for c in range(2):
            pl.semaphore_signal(barrier, inc=1, device_id={"tm": above + c})

    leave = leave_ref[...]
    stay = 1.0 - leave
    leave_col = jnp.transpose(jnp.broadcast_to(leave, (128, states)))
    for load in loads:
        load.wait()
    for r in range(nblk):
        total = jnp.sum(bw_ref[r, 0], axis=1, keepdims=True)
        for k in range(1, kb):
            total = total + jnp.sum(bw_ref[r, k], axis=1, keepdims=True)
        scale = leave_col[r * block:(r + 1) * block, :] / total
        for c in range(nblk):
            acc = bw_ref[r, 0] * jnp.where(cols_ref[0, r] == c, 1.0, 0.0)
            for k in range(1, kb):
                acc = acc + bw_ref[r, k] * jnp.where(cols_ref[k, r] == c, 1.0, 0.0)
            acc = acc * scale
            hi, lo = split(acc)
            rs = slice(r * block, (r + 1) * block)
            cs = slice(c * block, (c + 1) * block)
            w_ref[rs, cs] = acc
            w_hi[rs, cs] = hi
            w_lo[rs, cs] = lo

    em = em_ref[...]
    em = em / jnp.sum(em, axis=0, keepdims=True)
    e_ref[...] = jnp.zeros_like(e_ref)
    for j in range(per):
        for g in range(SUBS):
            s = sym_ref[g * per + j]
            row = jnp.zeros((1, states), f32)
            for v in range(symbols):
                row = row + em[v:v + 1] * jnp.where(s == v, 1.0, 0.0)
            e_ref[j, g:g + 1, :] = row

    eye = (lax.broadcasted_iota(jnp.int32, (states, states), 0)
           == lax.broadcasted_iota(jnp.int32, (states, states), 1))
    full_step = jnp.where(eye, jnp.broadcast_to(stay, (states, states)), 0.0) + w_ref[...]
    for g in range(SUBS):
        x_ref[g] = full_step * e_ref[0, g:g + 1, :]

    def advance(j, carry):
        for g in range(SUBS):
            x = x_ref[g]
            xb = x.astype(bf16)
            acc = dot(xb, w_hi[...]) + dot(xb, w_lo[...])
            x_ref[g] = (x * stay + acc) * e_ref[j, g:g + 1, :]
        return carry

    lax.fori_loop(1, per, advance, 0)

    for g in range(SUBS):
        x = x_ref[g]
        x = x * (1.0 / jnp.max(x))
        hi, lo = split(x)
        p_hi[g] = hi
        p_lo[g] = lo

    def joined(a, b):
        return dot(a[0], b[0]) + (dot(a[0], b[1]) + dot(a[1], b[0]))

    left = joined((p_hi[0], p_lo[0]), (p_hi[1], p_lo[1]))
    x_ref[0] = left
    right = joined((p_hi[2], p_lo[2]), (p_hi[3], p_lo[3]))
    x_ref[1] = right
    whole = joined(split(x_ref[0]), split(x_ref[1]))
    mine[...] = whole * (1.0 / jnp.max(whole))

    inner = jnp.logical_and(chip > 0, chip < chips - 1)

    @pl.when(inner)
    def _():
        pl.semaphore_wait(barrier, 5)

    @pl.when(jnp.logical_not(inner))
    def _():
        pl.semaphore_wait(barrier, 3)

    give_cols = pltpu.make_async_remote_copy(
        src_ref=mine.at[:, half:], dst_ref=got_cols, send_sem=x_send, recv_sem=x_recv,
        device_id={"tm": partner})
    give_rows = pltpu.make_async_remote_copy(
        src_ref=mine.at[:half, :], dst_ref=got_rows, send_sem=x_send, recv_sem=x_recv,
        device_id={"tm": partner})

    @pl.when(core == 0)
    def _():
        give_cols.start()

    @pl.when(core == 1)
    def _():
        give_rows.start()

    hi, lo = split(mine[...])
    h_hi[...] = hi
    h_lo[...] = lo

    @pl.when(core == 0)
    def _():
        give_rows.wait_recv()
        got = split(got_rows[...])
        hi, lo = split(joined((h_hi[:, :half], h_lo[:, :half]), got))
        q_hi[...] = hi
        q_lo[...] = lo

    @pl.when(core == 1)
    def _():
        give_cols.wait_recv()
        got = split(got_cols[...])
        hi, lo = split(joined(got, (h_hi[half:, :], h_lo[half:, :])))
        q_hi[...] = hi
        q_lo[...] = lo

    f_copies = [pltpu.make_async_remote_copy(
        src_ref=f_out, dst_ref=f_in.at[core], send_sem=f_send.at[c], recv_sem=f_recv.at[core],
        device_id={"tm": above + c}) for c in range(2)]
    b_copies = [pltpu.make_async_remote_copy(
        src_ref=b_out, dst_ref=b_in.at[core], send_sem=b_send.at[c], recv_sem=b_recv.at[core],
        device_id={"tm": below + c}) for c in range(2)]
    f_got = [pltpu.make_async_remote_copy(
        src_ref=f_out, dst_ref=f_in.at[c], send_sem=f_send.at[c], recv_sem=f_recv.at[c],
        device_id={"tm": above + c}) for c in range(2)]
    b_got = [pltpu.make_async_remote_copy(
        src_ref=b_out, dst_ref=b_in.at[c], send_sem=b_send.at[c], recv_sem=b_recv.at[c],
        device_id={"tm": below + c}) for c in range(2)]
    give_f = pltpu.make_async_remote_copy(
        src_ref=side_out, dst_ref=f_side, send_sem=s_send, recv_sem=s_recv,
        device_id={"tm": partner})
    give_b = pltpu.make_async_remote_copy(
        src_ref=side_out, dst_ref=b_side, send_sem=s_send, recv_sem=s_recv,
        device_id={"tm": partner})

    def forward_hop():
        @pl.when(chip == 0)
        def _():
            f_in[0] = init_ref[...]
            f_in[1] = jnp.zeros((1, states), f32)

        @pl.when(chip > 0)
        def _():
            for got in f_got:
                got.wait_recv()

        @pl.when(chip < chips - 1)
        def _():
            v = f_in[0] + f_in[1]
            out = thin(jnp.broadcast_to(v, (8, states)), q_hi[...], q_lo[...])
            f_out[...] = out[0:1] * (1.0 / jnp.sum(v))
            for copy in f_copies:
                copy.start()

        @pl.when(core == 0)
        def _():
            v = f_in[0] + f_in[1]
            out = thin(jnp.broadcast_to(v, (8, states)), h_hi[...], h_lo[...])
            side_out[...] = out[0:1] * (1.0 / jnp.sum(v))
            give_f.start()

    def backward_hop():
        @pl.when(chip == chips - 1)
        def _():
            b_in[0] = jnp.full((1, states), 1.0 / states, f32)
            b_in[1] = jnp.zeros((1, states), f32)

        @pl.when(chip < chips - 1)
        def _():
            for got in b_got:
                got.wait_recv()

        @pl.when(chip > 0)
        def _():
            w = b_in[0] + b_in[1]
            out = thin(jnp.broadcast_to(w, (8, states)), q_hi[...], q_lo[...], NT)
            b_out[...] = out[0:1] * (1.0 / jnp.sum(w))
            for copy in b_copies:
                copy.start()

        @pl.when(core == 1)
        def _():
            w = b_in[0] + b_in[1]
            out = thin(jnp.broadcast_to(w, (8, states)), h_hi[...], h_lo[...], NT)
            side_out[...] = out[0:1] * (1.0 / jnp.sum(w))
            give_b.start()

    @pl.when(2 * chip < chips)
    def _():
        forward_hop()
        backward_hop()

    @pl.when(2 * chip >= chips)
    def _():
        backward_hop()
        forward_hop()

    @pl.when(core == 0)
    def _():
        f_side[...] = f_in[0] + f_in[1]
        give_b.wait_recv()

    @pl.when(core == 1)
    def _():
        b_side[...] = b_in[0] + b_in[1]
        give_f.wait_recv()

    def unit(x):
        return x * (1.0 / jnp.sum(x, axis=1, keepdims=True))

    fs = [unit(f_side[...])]
    for g in range(SUBS - 1):
        nxt = thin(jnp.broadcast_to(fs[-1], (8, states)), p_hi[g], p_lo[g])
        fs.append(unit(nxt[0:1]))
    bs = [unit(b_side[...])]
    for g in range(SUBS - 1, 0, -1):
        nxt = thin(jnp.broadcast_to(bs[-1], (8, states)), p_hi[g], p_lo[g], NT)
        bs.append(unit(nxt[0:1]))
    bs = bs[::-1]
    pad = [jnp.zeros((8 - SUBS, states), f32)]
    f = jnp.concatenate(fs + pad, axis=0)
    b = jnp.concatenate(bs + pad, axis=0)
    b_ref[per - 1] = b
    for i in range(per):
        f = (f * stay + thin(f, w_hi[...], w_lo[...])) * e_ref[i]
        u_ref[i] = f
        j = per - 1 - i
        if j > 0:
            m = b * e_ref[j]
            b = m * stay + thin(m, w_hi[...], w_lo[...], NT)
            b_ref[j - 1] = b

    l_ref[...] = jnp.zeros_like(l_ref)
    before = jnp.ones((8, 1), f32)
    for i in range(per):
        u = u_ref[i]
        here = jnp.sum(u, axis=1, keepdims=True)
        logs = jnp.log(here / before)
        before = here
        bb = b_ref[i]
        joint = (u / here) * (bb / jnp.sum(bb, axis=1, keepdims=True))
        occ = states * joint / jnp.sum(joint, axis=1, keepdims=True)
        for g in range(SUBS):
            occ_ref[g * per + i:g * per + i + 1, :] = occ[g:g + 1]
            l_ref[g * per + i:g * per + i + 1, :] = jnp.broadcast_to(logs[g:g + 1], (1, 128))

    ln_ref[...] = jnp.transpose(l_ref[...])[0:1, :steps]

    @pl.when(chip < chips - 1)
    def _():
        for copy in f_copies:
            copy.wait_send()

    @pl.when(chip > 0)
    def _():
        for copy in b_copies:
            copy.wait_send()

    @pl.when(core == 0)
    def _():
        give_cols.wait_send()
        give_f.wait_send()

    @pl.when(core == 1)
    def _():
        give_rows.wait_send()
        give_b.wait_send()


def body(initial_weights, leave_rate, block_weights, block_cols, emission_weights, symbols):
    states = leave_rate.shape[0]
    steps = symbols.shape[0]
    per = steps // SUBS
    vmem = pl.BlockSpec(memory_space=pltpu.VMEM)
    far = pl.BlockSpec(memory_space=pltpu.HBM)
    dma = pltpu.SemaphoreType.DMA
    tall = -(-steps // 128) * 128
    square = (states, states)
    row = pltpu.VMEM((1, states), f32)
    pair = pltpu.VMEM((2, 1, states), f32)
    occupancy, log_norm = pl.pallas_call(
        kernel,
        out_shape=(jax.ShapeDtypeStruct((steps, states), f32),
                   jax.ShapeDtypeStruct((1, steps), f32)),
        in_specs=[vmem, vmem, far, far, far, far],
        out_specs=(vmem, vmem),
        scratch_shapes=[
            pltpu.VMEM(block_weights.shape, f32), pltpu.SMEM(block_cols.shape[::-1], jnp.int32),
            pltpu.VMEM(emission_weights.shape, f32), pltpu.SMEM(symbols.shape, jnp.int32), dma((4,)),
            pltpu.VMEM(square, f32), pltpu.VMEM(square, bf16), pltpu.VMEM(square, bf16),
            pltpu.VMEM((SUBS,) + square, f32),
            pltpu.VMEM((SUBS,) + square, bf16), pltpu.VMEM((SUBS,) + square, bf16),
            pltpu.VMEM(square, bf16), pltpu.VMEM(square, bf16),
            pltpu.VMEM(square, bf16), pltpu.VMEM(square, bf16),
            pltpu.VMEM((per, 8, states), f32), pltpu.VMEM((per, 8, states), f32),
            pltpu.VMEM((per, 8, states), f32), pltpu.VMEM((tall, 128), f32),
            pltpu.VMEM(square, f32), pltpu.VMEM((states, states // 2), f32),
            pltpu.VMEM((states // 2, states), f32),
            pair, row, pair, row, row, row, row,
            dma, dma, dma((2,)), dma((2,)), dma((2,)), dma((2,)), dma, dma,
        ],
        compiler_params=pltpu.CompilerParams(
            collective_id=0, has_side_effects=True, vmem_limit_bytes=48 * 1024 * 1024),
    )(initial_weights[None, :], leave_rate[None, :], block_weights, block_cols.T,
      emission_weights, symbols)
    return occupancy, log_norm[0]


def solution(mesh):
    placed = (P(), P(), P(), P(), P(), P(("grp", "tm")))
    return jax.shard_map(
        body,
        mesh=mesh,
        in_specs=placed,
        out_specs=(P(("grp", "tm"), None), P(("grp", "tm"))),
        check_vma=False,
    )
```

time: 59.7 us -> 54.8 us (0.918)
  Pallas kernels: 54.5 us -> 50.4 us
  other arithmetic: 0.63 us -> 0 us
    pallas_call x1, Pallas kernels: 54.5 us -> 50.4 us  [body(): pl.pallas_call(kernel, out_shape=(jax.ShapeDtypeStruct((steps, states), f...]
    pallas_call x1 -> x0, other arithmetic: 0.63 us -> none  [body(): pl.pallas_call(kernel, out_shape=(jax.ShapeDtypeStruct((steps, states), f...]
where the time goes in v2:
time: 54.8 us; the launch traced here: 54.6 us
  Pallas kernels  50.4 us (92%)
  local copies, waits for them, and re-layouts  3.55 us (6%)
  between operations  0.68 us (1%)
    pallas_call x1, Pallas kernels, body(): pl.pallas_call(kernel, out_shape=(jax.ShapeDtypeStruct((steps, states), f...  50.4 us
    unnamed x14, local copies, waits for them, and re-layouts  3.55 us

profile of v2, /device:TPU:0, one launch (start us, length us, event | category | flops | bytes accessed | tf_op | source)
XLA Modules:
  0.0 54.6 jit_solution(15913637881953395145)
XLA Ops:
  0.6 0.0 copy-start.3
  0.6 0.0 copy-start.2
  0.7 0.0 copy-start.4
  0.7 0.0 copy-start.5
  0.7 0.6 %copy-done.3 = f32[512]{0:T(512)S(1)} copy-done((f32[512]{0:T(512)S(1)}, f32[512]{0:T(512)}, u32[]{:S(2)}) %copy-start.3) | copy-done | bytes 2072
  1.3 0.0 copy-done.2
  1.3 0.0 copy-done.4
  1.3 0.0 copy-done.5
  1.3 0.0 copy-start
  1.3 1.0 %copy-done = f32[4,2,128,128]{3,2,1,0:T(8,128)S(1)} copy-done((f32[4,2,128,128]{3,2,1,0:T(8,128)S(1)}, f32[4,2,128,128]{3,2,1,0:T(8,128)}, u32[]{:S(2)}) %copy-start) | copy-done | bytes 524312
  2.4 0.0 copy-start.1
  2.4 0.7 %copy-done.1 = f32[4,512]{1,0:T(4,128)S(1)} copy-done((f32[4,512]{1,0:T(4,128)S(1)}, f32[4,512]{1,0:T(4,128)}, u32[]{:S(2)}) %copy-start.1) | copy-done | bytes 8216
  3.1 50.4 %shard_map.77 = (f32[24,512]{1,0:T(8,128)S(1)}, f32[1,24]{1,0:T(1,128)S(1)}) custom-call(f32[1,512]{1,0:T(1,128)S(1)} %bitcast.4, f32[1,512]{1,0:T(1,128)S(1)} %bitcast.5, f32[4,2,128,128]{3,2,1,0:T(8,128)S(1)} %copy-done, s32[2,4]{1,0:T(2,128)S(1)} %bitcast.6, f32[4,512]{1,0:T(4,128)S(1)} %copy-done.1, s32[24]{0:T(128)S(1)} %copy-done.5), custom_call_target="tpu_custom_call" | custom-call | tf_op jit(solution)/shard_map/pallas_call | solution.py:347
  53.5 0.6 %copy.10 = f32[24,512]{1,0:T(8,128)} copy(f32[24,512]{1,0:T(8,128)S(1)} %get-tuple-element.8) | data formatting | bytes 98304
  54.1 0.5 copy.11
Async XLA Ops:
  0.6 0.7 %copy-start.3 = (f32[512]{0:T(512)S(1)}, f32[512]{0:T(512)}, u32[]{:S(2)}) copy-start(f32[512]{0:T(512)} %param.7) | copy-start | bytes 6148
  0.6 0.7 %copy-start.2 = (f32[512]{0:T(512)S(1)}, f32[512]{0:T(512)}, u32[]{:S(2)}) copy-start(f32[512]{0:T(512)} %param.6) | copy-start | bytes 6148
  0.7 0.7 %copy-start.4 = (s32[4,2]{0,1:T(2,128)S(1)}, s32[4,2]{0,1:T(2,128)}, u32[]{:S(2)}) copy-start(s32[4,2]{0,1:T(2,128)} %param.9) | copy-start | bytes 100
  0.7 0.7 %copy-start.5 = (s32[24]{0:T(128)S(1)}, s32[24]{0:T(128)}, u32[]{:S(2)}) copy-start(s32[24]{0:T(128)} %sym_hbm.1) | copy-start | bytes 292
  1.3 1.0 %copy-start = (f32[4,2,128,128]{3,2,1,0:T(8,128)S(1)}, f32[4,2,128,128]{3,2,1,0:T(8,128)}, u32[]{:S(2)}) copy-start(f32[4,2,128,128]{3,2,1,0:T(8,128)} %bw_hbm.1) | copy-start | bytes 1572868
  2.4 0.7 %copy-start.1 = (f32[4,512]{1,0:T(4,128)S(1)}, f32[4,512]{1,0:T(4,128)}, u32[]{:S(2)}) copy-start(f32[4,512]{1,0:T(4,128)} %em_hbm.1) | copy-start | bytes 24580

commit v3 on v2

--- a/solution.py
+++ b/solution.py
@@ -10,7 +10,6 @@
 bf16 = jnp.bfloat16
 SUBS = 4
 NN = (((1,), (0,)), ((), ()))
-NT = (((1,), (1,)), ((), ()))
 
 
 def split(x):
@@ -18,21 +17,22 @@
     return hi, (x - hi.astype(f32)).astype(bf16)
 
 
-def dot(a, b, dims=NN):
-    return lax.dot_general(a, b, dims, preferred_element_type=f32)
-
-
-def thin(x, hi, lo, dims=NN):
+def dot(a, b):
+    return lax.dot_general(a, b, NN, preferred_element_type=f32)
+
+
+def thin(x, hi, lo):
     top = x.astype(bf16).astype(f32)
     both = jnp.concatenate([top, x - top], axis=0).astype(bf16)
-    first = dot(both, hi, dims)
-    second = dot(both, lo, dims)
+    first = dot(both, hi)
+    second = dot(both, lo)
     return first[:8] + (first[8:] + second[:8])
 
 
 def kernel(init_ref, leave_ref, bw_hbm, cols_hbm, em_hbm, sym_hbm, occ_ref, ln_ref,
            bw_ref, cols_ref, em_ref, sym_ref, in_sems,
-           w_ref, w_hi, w_lo, x_ref, p_hi, p_lo, h_hi, h_lo, q_hi, q_lo, e_ref, u_ref, b_ref, l_ref,
+           w_ref, w_hi, w_lo, x_ref, p_hi, p_lo, h_hi, h_lo, q_hi, q_lo,
+           wt_hi, wt_lo, pt_hi, pt_lo, ht_hi, ht_lo, qt_hi, qt_lo, e_ref, u_ref, b_ref, l_ref,
            mine, got_cols, got_rows, f_in, f_out, b_in, b_out, f_side, b_side, side_out,
            x_send, x_recv, f_send, f_recv, b_send, b_recv, s_send, s_recv):
     pos = lax.axis_index("tm")
@@ -129,10 +129,10 @@
         return dot(a[0], b[0]) + (dot(a[0], b[1]) + dot(a[1], b[0]))
 
     left = joined((p_hi[0], p_lo[0]), (p_hi[1], p_lo[1]))
-    x_ref[0] = left
+    x_ref[SUBS] = left
     right = joined((p_hi[2], p_lo[2]), (p_hi[3], p_lo[3]))
-    x_ref[1] = right
-    whole = joined(split(x_ref[0]), split(x_ref[1]))
+    x_ref[SUBS + 1] = right
+    whole = joined(split(x_ref[SUBS]), split(x_ref[SUBS + 1]))
     mine[...] = whole * (1.0 / jnp.max(whole))
 
     inner = jnp.logical_and(chip > 0, chip < chips - 1)
@@ -163,22 +163,38 @@
     hi, lo = split(mine[...])
     h_hi[...] = hi
     h_lo[...] = lo
+    hi, lo = split(jnp.transpose(w_ref[...]))
+    wt_hi[...] = hi
+    wt_lo[...] = lo
+    for g in range(1, SUBS):
+        hi, lo = split(jnp.transpose(x_ref[g]))
+        pt_hi[g] = hi
+        pt_lo[g] = lo
+
+    @pl.when(core == 1)
+    def _():
+        hi, lo = split(jnp.transpose(mine[...]))
+        ht_hi[...] = hi
+        ht_lo[...] = lo
 
     @pl.when(core == 0)
     def _():
         give_rows.wait_recv()
         got = split(got_rows[...])
-        hi, lo = split(joined((h_hi[:, :half], h_lo[:, :half]), got))
-        q_hi[...] = hi
-        q_lo[...] = lo
+        x_ref[SUBS] = joined((h_hi[:, :half], h_lo[:, :half]), got)
 
     @pl.when(core == 1)
     def _():
         give_cols.wait_recv()
         got = split(got_cols[...])
-        hi, lo = split(joined(got, (h_hi[half:, :], h_lo[half:, :])))
-        q_hi[...] = hi
-        q_lo[...] = lo
+        x_ref[SUBS] = joined(got, (h_hi[half:, :], h_lo[half:, :]))
+
+    hi, lo = split(x_ref[SUBS])
+    q_hi[...] = hi
+    q_lo[...] = lo
+    hi, lo = split(jnp.transpose(x_ref[SUBS]))
+    qt_hi[...] = hi
+    qt_lo[...] = lo
 
     f_copies = [pltpu.make_async_remote_copy(
         src_ref=f_out, dst_ref=f_in.at[core], send_sem=f_send.at[c], recv_sem=f_recv.at[core],
@@ -239,7 +255,7 @@
         @pl.when(chip > 0)
         def _():
             w = b_in[0] + b_in[1]
-            out = thin(jnp.broadcast_to(w, (8, states)), q_hi[...], q_lo[...], NT)
+            out = thin(jnp.broadcast_to(w, (8, states)), qt_hi[...], qt_lo[...])
             b_out[...] = out[0:1] * (1.0 / jnp.sum(w))
             for copy in b_copies:
                 copy.start()
@@ -247,7 +263,7 @@
         @pl.when(core == 1)
         def _():
             w = b_in[0] + b_in[1]
-            out = thin(jnp.broadcast_to(w, (8, states)), h_hi[...], h_lo[...], NT)
+            out = thin(jnp.broadcast_to(w, (8, states)), ht_hi[...], ht_lo[...])
             side_out[...] = out[0:1] * (1.0 / jnp.sum(w))
             give_b.start()
 
@@ -280,7 +296,7 @@
         fs.append(unit(nxt[0:1]))
     bs = [unit(b_side[...])]
     for g in range(SUBS - 1, 0, -1):
-        nxt = thin(jnp.broadcast_to(bs[-1], (8, states)), p_hi[g], p_lo[g], NT)
+        nxt = thin(jnp.broadcast_to(bs[-1], (8, states)), pt_hi[g], pt_lo[g])
         bs.append(unit(nxt[0:1]))
     bs = bs[::-1]
     pad = [jnp.zeros((8 - SUBS, states), f32)]
@@ -293,7 +309,7 @@
         j = per - 1 - i
         if j > 0:
             m = b * e_ref[j]
-            b = m * stay + thin(m, w_hi[...], w_lo[...], NT)
+            b = m * stay + thin(m, wt_hi[...], wt_lo[...])
             b_ref[j - 1] = b
 
     l_ref[...] = jnp.zeros_like(l_ref)
@@ -354,7 +370,11 @@
             pltpu.VMEM(block_weights.shape, f32), pltpu.SMEM(block_cols.shape[::-1], jnp.int32),
             pltpu.VMEM(emission_weights.shape, f32), pltpu.SMEM(symbols.shape, jnp.int32), dma((4,)),
             pltpu.VMEM(square, f32), pltpu.VMEM(square, bf16), pltpu.VMEM(square, bf16),
-            pltpu.VMEM((SUBS,) + square, f32),
+            pltpu.VMEM((SUBS + 2,) + square, f32),
+            pltpu.VMEM((SUBS,) + square, bf16), pltpu.VMEM((SUBS,) + square, bf16),
+            pltpu.VMEM(square, bf16), pltpu.VMEM(square, bf16),
+            pltpu.VMEM(square, bf16), pltpu.VMEM(square, bf16),
+            pltpu.VMEM(square, bf16), pltpu.VMEM(square, bf16),
             pltpu.VMEM((SUBS,) + square, bf16), pltpu.VMEM((SUBS,) + square, bf16),
             pltpu.VMEM(square, bf16), pltpu.VMEM(square, bf16),
             pltpu.VMEM(square, bf16), pltpu.VMEM(square, bf16),
@@ -366,7 +386,7 @@
             dma, dma, dma((2,)), dma((2,)), dma((2,)), dma((2,)), dma, dma,
         ],
         compiler_params=pltpu.CompilerParams(
-            collective_id=0, has_side_effects=True, vmem_limit_bytes=48 * 1024 * 1024),
+            collective_id=0, has_side_effects=True, vmem_limit_bytes=64 * 1024 * 1024 - 65536),
     )(initial_weights[None, :], leave_rate[None, :], block_weights, block_cols.T,
       emission_weights, symbols)
     return occupancy, log_norm[0]

time: 54.8 us -> 53.5 us (0.976)
  local copies, waits for them, and re-layouts: 3.55 us -> 1.94 us
    unnamed x14 -> x4, local copies, waits for them, and re-layouts: 3.55 us -> 1.94 us
where the time goes in v3:
time: 53.5 us; the launch traced here: 53.2 us
  Pallas kernels  50.7 us (95%)
  local copies, waits for them, and re-layouts  1.94 us (4%)
  between operations  0.65 us (1%)
    pallas_call x1, Pallas kernels, body(): pl.pallas_call(kernel, out_shape=(jax.ShapeDtypeStruct((steps, states), f...  50.7 us
    unnamed x4, local copies, waits for them, and re-layouts  1.94 us

profile of v3, /device:TPU:0, one launch (start us, length us, event | category | flops | bytes accessed | tf_op | source)
XLA Modules:
  0.0 53.2 jit_solution(1524943336668759435)
XLA Ops:
  0.6 50.7 %shard_map.77 = (f32[24,512]{1,0:T(8,128)}, f32[1,24]{1,0:T(1,128)}) custom-call(f32[1,512]{1,0:T(1,128)} %bitcast.4, f32[1,512]{1,0:T(1,128)} %bitcast.5, f32[4,2,128,128]{3,2,1,0:T(8,128)} %bw_hbm.1, s32[2,4]{1,0:T(2,128)} %bitcast.6, f32[4,512]{1,0:T(4,128)} %em_hbm.1, s32[24]{0:T(128)} %sym_hbm.1), custom_call_target="tpu_custom_call" | custom-call | tf_op jit(solution)/shard_map/pallas_call | solution.py:363
  51.3 0.0 copy-start
  51.3 1.4 %copy.10 = f32[24,512]{1,0:T(8,128)} copy(f32[24,512]{1,0:T(8,128)} %get-tuple-element.8) | data formatting | bytes 98304
  52.7 0.0 copy-done
  52.7 0.5 copy.11
Async XLA Ops:
  51.3 1.4 %copy-start = (f32[1,24]{1,0:T(1,128)S(1)}, f32[1,24]{1,0:T(1,128)}, u32[]{:S(2)}) copy-start(f32[1,24]{1,0:T(1,128)} %get-tuple-element.5) | copy-start | bytes 292

commit v4 on v3

--- a/solution.py
+++ b/solution.py
@@ -108,15 +108,25 @@
     for g in range(SUBS):
         x_ref[g] = full_step * e_ref[0, g:g + 1, :]
 
-    def advance(j, carry):
+    def advance(j, low):
         for g in range(SUBS):
             x = x_ref[g]
             xb = x.astype(bf16)
-            acc = dot(xb, w_hi[...]) + dot(xb, w_lo[...])
+            acc = dot(xb, w_hi[...])
+            if low:
+                acc = acc + low * dot(xb, w_lo[...])
             x_ref[g] = (x * stay + acc) * e_ref[j, g:g + 1, :]
+
+    pairs = max(per - 2, 0) // 2
+
+    def advance_pair(i, carry):
+        advance(2 * i + 1, 0)
+        advance(2 * i + 2, 2.0)
         return carry
 
-    lax.fori_loop(1, per, advance, 0)
+    lax.fori_loop(0, pairs, advance_pair, 0)
+    for j in range(2 * pairs + 1, per):
+        advance(j, 1.0)
 
     for g in range(SUBS):
         x = x_ref[g]

time: 53.5 us -> 50.7 us (0.948)
  Pallas kernels: 50.7 us -> 47.9 us
    pallas_call x1, Pallas kernels: 50.7 us -> 47.9 us  [body(): pl.pallas_call(kernel, out_shape=(jax.ShapeDtypeStruct((steps, states), f...]
where the time goes in v4:
time: 50.7 us; the launch traced here: 50.5 us
  Pallas kernels  47.9 us (94%)
  local copies, waits for them, and re-layouts  1.94 us (4%)
  between operations  0.65 us (1%)
    pallas_call x1, Pallas kernels, body(): pl.pallas_call(kernel, out_shape=(jax.ShapeDtypeStruct((steps, states), f...  47.9 us
    unnamed x4, local copies, waits for them, and re-layouts  1.94 us

profile of v4, /device:TPU:0, one launch (start us, length us, event | category | flops | bytes accessed | tf_op | source)
XLA Modules:
  0.0 50.5 jit_solution(7241896811747198048)
XLA Ops:
  0.6 47.9 %shard_map.77 = (f32[24,512]{1,0:T(8,128)}, f32[1,24]{1,0:T(1,128)}) custom-call(f32[1,512]{1,0:T(1,128)} %bitcast.4, f32[1,512]{1,0:T(1,128)} %bitcast.5, f32[4,2,128,128]{3,2,1,0:T(8,128)} %bw_hbm.1, s32[2,4]{1,0:T(2,128)} %bitcast.6, f32[4,512]{1,0:T(4,128)} %em_hbm.1, s32[24]{0:T(128)} %sym_hbm.1), custom_call_target="tpu_custom_call" | custom-call | tf_op jit(solution)/shard_map/pallas_call | solution.py:373
  48.5 0.0 copy-start
  48.5 1.4 %copy.10 = f32[24,512]{1,0:T(8,128)} copy(f32[24,512]{1,0:T(8,128)} %get-tuple-element.8) | data formatting | bytes 98304
  49.9 0.0 copy-done
  49.9 0.5 %copy.11 = f32[24]{0:T(128)} copy(f32[24]{0:T(128)S(1)} %bitcast.7) | data formatting | bytes 192
Async XLA Ops:
  48.5 1.4 %copy-start = (f32[1,24]{1,0:T(1,128)S(1)}, f32[1,24]{1,0:T(1,128)}, u32[]{:S(2)}) copy-start(f32[1,24]{1,0:T(1,128)} %get-tuple-element.5) | copy-start | bytes 292

commit v5 on v4

--- a/solution.py
+++ b/solution.py
@@ -240,7 +240,7 @@
         def _():
             v = f_in[0] + f_in[1]
             out = thin(jnp.broadcast_to(v, (8, states)), q_hi[...], q_lo[...])
-            f_out[...] = out[0:1] * (1.0 / jnp.sum(v))
+            f_out[...] = out[0:1] * (1.0 / jnp.sum(v, axis=1, keepdims=True))
             for copy in f_copies:
                 copy.start()
 
@@ -248,7 +248,7 @@
         def _():
             v = f_in[0] + f_in[1]
             out = thin(jnp.broadcast_to(v, (8, states)), h_hi[...], h_lo[...])
-            side_out[...] = out[0:1] * (1.0 / jnp.sum(v))
+            side_out[...] = out[0:1] * (1.0 / jnp.sum(v, axis=1, keepdims=True))
             give_f.start()
 
     def backward_hop():
@@ -266,7 +266,7 @@
         def _():
             w = b_in[0] + b_in[1]
             out = thin(jnp.broadcast_to(w, (8, states)), qt_hi[...], qt_lo[...])
-            b_out[...] = out[0:1] * (1.0 / jnp.sum(w))
+            b_out[...] = out[0:1] * (1.0 / jnp.sum(w, axis=1, keepdims=True))
             for copy in b_copies:
                 copy.start()
 
@@ -274,7 +274,7 @@
         def _():
             w = b_in[0] + b_in[1]
             out = thin(jnp.broadcast_to(w, (8, states)), ht_hi[...], ht_lo[...])
-            side_out[...] = out[0:1] * (1.0 / jnp.sum(w))
+            side_out[...] = out[0:1] * (1.0 / jnp.sum(w, axis=1, keepdims=True))
             give_b.start()
 
     @pl.when(2 * chip < chips)

time: 50.7 us -> 50.6 us (level)
  no operation moved by 1% of the time
where the time goes in v5:
time: 50.6 us; the launch traced here: 50.4 us
  Pallas kernels  47.8 us (94%)
  local copies, waits for them, and re-layouts  1.94 us (4%)
  between operations  0.65 us (1%)
    pallas_call x1, Pallas kernels, body(): pl.pallas_call(kernel, out_shape=(jax.ShapeDtypeStruct((steps, states), f...  47.8 us
    unnamed x4, local copies, waits for them, and re-layouts  1.94 us

profile of v5, /device:TPU:0, one launch (start us, length us, event | category | flops | bytes accessed | tf_op | source)
XLA Modules:
  0.0 50.4 jit_solution(18214709346669388613)
XLA Ops:
  0.6 47.8 %shard_map.77 = (f32[24,512]{1,0:T(8,128)}, f32[1,24]{1,0:T(1,128)}) custom-call(f32[1,512]{1,0:T(1,128)} %bitcast.4, f32[1,512]{1,0:T(1,128)} %bitcast.5, f32[4,2,128,128]{3,2,1,0:T(8,128)} %bw_hbm.1, s32[2,4]{1,0:T(2,128)} %bitcast.6, f32[4,512]{1,0:T(4,128)} %em_hbm.1, s32[24]{0:T(128)} %sym_hbm.1), custom_call_target="tpu_custom_call" | custom-call | tf_op jit(solution)/shard_map/pallas_call | solution.py:373
  48.5 0.0 copy-start
  48.5 1.4 %copy.10 = f32[24,512]{1,0:T(8,128)} copy(f32[24,512]{1,0:T(8,128)} %get-tuple-element.8) | data formatting | bytes 98304
  49.9 0.0 copy-done
  49.9 0.5 %copy.11 = f32[24]{0:T(128)} copy(f32[24]{0:T(128)S(1)} %bitcast.7) | data formatting | bytes 192
Async XLA Ops:
  48.5 1.4 %copy-start = (f32[1,24]{1,0:T(1,128)S(1)}, f32[1,24]{1,0:T(1,128)}, u32[]{:S(2)}) copy-start(f32[1,24]{1,0:T(1,128)} %get-tuple-element.5) | copy-start | bytes 292
